TPU v7x, 32 devices: a whole 2x2x4 slice. The times are simulated.
32 devices in a mesh: groups: 2 (over y), seq: 8 (over z, x), head: 2 (over core).
Axes of the slice: x: 2, y: 2, z: 4, core: 2. Of those that a mesh axis runs over, the one named last changes fastest.
Arguments:
- text_query_rows: bfloat16 [2048, 8192], P(('groups', 'seq'), 'head'), parts along dimension 0, may hold values from -40 to 40, as said below
- text_key_value: bfloat16 [2, 2048, 1024], P(None, ('groups', 'seq'), 'head'), parts along dimension 1, may hold values from -4 to 4, as said below
- doc_ids: int32 [2048], P(('groups', 'seq')), parts along dimension 0, may hold values from 0 to 3, never falling along the last dimension, each value on 1 to 512 neighbouring positions
- tile_span: int32 [2048, 2], P(('groups', 'seq')), parts along dimension 0, may hold values from 0 to 8, as said below
- vision_hidden: bfloat16 [4096, 1280], P(('groups', 'seq')), parts along dimension 0, may hold values from -6 to 6
- vision_qkv: bfloat16 [3, 4096, 1280], P(None, ('groups', 'seq'), 'head'), parts along dimension 1, may hold values from -6 to 6, as said below
- vision_out_weight: bfloat16 [1280, 1280], P('head'), may hold values from -0.625 to 0.625
- cross_keyvalue_weight: bfloat16 [1280, 2, 1024], P('seq', None, 'head'), may hold values from -0.15625 to 0.15625
- cross_gate: float32 [64], P('head'), may hold values from -1.5 to 1.5
Outputs:
- attention_out: bfloat16 [2048, 8192], P(('groups', 'seq'), 'head'), parts along dimension 0
There are 2 independent parts, one for each index of `groups`. A program takes and returns all parts, laid end to end along the dimension named above; an argument that names none is the same for every part. Nothing has to cross between parts.
Inputs may be any that keep to these rules, and one draw needn't show every extreme that they name: `tile_span`: each text token's span is an interval of the tiles of its own block b = p // 128 and of block b - 1 (first <= second, both between b - 1 and b + 1, never below 0); it may be empty. `doc_ids`: never falling along the document; each segment holds 1 to 512 tokens. `text_query_rows`: real values. `text_key_value`: real values. `vision_qkv`: real values.
All inputs are finite; a program needn't handle non-finite values.
Results may differ from a plain program's by a relative error of at most 0.024.
Values may be sent and summed in bfloat16 or wider, within the bound.
A program may use at most 64 MiB of HBM per device.

v0:
```python
import math
import jax
import jax.numpy as jnp
from jax import lax
from jax.sharding import PartitionSpec as P

HEAD_SIZE = 128
VHD = 80
WINDOW_BLOCKS = 2


def passed_along(block, axis, distance):
    devices = range(lax.axis_size(axis))
    route = [(i - distance, i) for i in devices if i - distance in devices]
    return lax.ppermute(block, axis, route)


def attend_heads(query_rows, keys, allowed_mask):
    scores = jnp.einsum(
        "tgrd,kgd->grtk", query_rows, keys, preferred_element_type=jnp.float32
    ) / math.sqrt(HEAD_SIZE)
    scores = jnp.where(allowed_mask[None, None], scores, -1e30)
    return jax.nn.softmax(scores, axis=-1)


def per_device(
    text_query_rows,
    text_key_value,
    doc_ids,
    tile_span,
    vision_hidden,
    vision_qkv,
    vision_out_weight,
    cross_keyvalue_weight,
    cross_gate,
):
    text_rows = text_query_rows.shape[0]
    tile_rows = vision_hidden.shape[0]
    kv_cols = text_key_value.shape[2]
    kv_heads = kv_cols // HEAD_SIZE
    query_group_ratio = text_query_rows.shape[1] // HEAD_SIZE // kv_heads
    seq_index = lax.axis_index("seq")
    vision_query = vision_qkv[0].reshape(tile_rows, -1, VHD)
    vision_key = vision_qkv[1].reshape(tile_rows, -1, VHD)
    vision_value = vision_qkv[2].reshape(tile_rows, -1, VHD)
    vision_scores = jnp.einsum(
        "qhd,khd->hqk", vision_query, vision_key, preferred_element_type=jnp.float32
    ) / math.sqrt(VHD)
    vision_weights = jax.nn.softmax(vision_scores, axis=-1).astype(jnp.bfloat16)
    vision_attn = jnp.einsum(
        "hqk,khd->qhd", vision_weights, vision_value, preferred_element_type=jnp.float32
    )
    vision_attn = vision_attn.astype(jnp.bfloat16).reshape(tile_rows, -1)
    partial_mix = jnp.dot(vision_attn, vision_out_weight, preferred_element_type=jnp.float32)
    mixed_sum = lax.psum(partial_mix, "head") + vision_hidden.astype(jnp.float32)
    image_norm = (
        mixed_sum * lax.rsqrt(jnp.mean(mixed_sum * mixed_sum, axis=-1, keepdims=True) + 1e-05)
    ).astype(jnp.bfloat16)
    image_key_value = jnp.einsum(
        "ic,cjf->ijf",
        image_norm,
        lax.all_gather(cross_keyvalue_weight, "seq", axis=0, tiled=True),
        preferred_element_type=jnp.float32,
    ).astype(jnp.bfloat16)
    earlier_tile = passed_along(image_key_value, "seq", 1)
    blocks = [(text_key_value, doc_ids)]
    current_kv, current_docs = (text_key_value, doc_ids)
    for repeat_count in range(WINDOW_BLOCKS):
        current_kv, current_docs = passed_along((current_kv, current_docs), "seq", 1)
        blocks.insert(0, (current_kv, current_docs))
    all_keyval = jnp.concatenate([member[0] for member in blocks], axis=1)
    all_docs = jnp.concatenate([member[1] for member in blocks], axis=0)
    key_pos = (seq_index - WINDOW_BLOCKS) * text_rows + jnp.arange(
        (WINDOW_BLOCKS + 1) * text_rows, dtype=jnp.int32
    )
    query_pos = seq_index * text_rows + jnp.arange(text_rows, dtype=jnp.int32)
    allowed_mask = (
        (all_docs[None, :] == doc_ids[:, None])
        & (key_pos[None, :] <= query_pos[:, None])
        & (key_pos[None, :] >= 0)
    )
    query_rows = text_query_rows.reshape(text_rows, kv_heads, query_group_ratio, HEAD_SIZE)
    self_attention_weights = attend_heads(
        query_rows, all_keyval[0].reshape(-1, kv_heads, HEAD_SIZE), allowed_mask
    ).astype(jnp.bfloat16)
    self_output = jnp.einsum(
        "ycmq,qyb->mycb",
        self_attention_weights,
        all_keyval[1].reshape(-1, kv_heads, HEAD_SIZE),
        preferred_element_type=jnp.float32,
    )
    self_output = self_output.reshape(text_rows, -1)
    image_all = jnp.concatenate([earlier_tile, image_key_value], axis=0)
    tile_ids = seq_index - 1 + jnp.arange(2 * tile_rows, dtype=jnp.int32) // tile_rows
    low_tile = tile_span[:, 0]
    high_tile = tile_span[:, 1]
    visible_mask = (tile_ids[None, :] >= low_tile[:, None]) & (
        tile_ids[None, :] < high_tile[:, None]
    )
    image_present = (high_tile > low_tile).astype(jnp.float32)
    cross_probabilities = (
        attend_heads(query_rows, image_all[:, 0].reshape(-1, kv_heads, HEAD_SIZE), visible_mask)
        * image_present[None, None, :, None]
    )
    cross_probabilities = cross_probabilities.astype(jnp.bfloat16)
    cross_output = jnp.einsum(
        "ycmq,qyb->mycb",
        cross_probabilities,
        image_all[:, 1].reshape(-1, kv_heads, HEAD_SIZE),
        preferred_element_type=jnp.float32,
    )
    cross_output = cross_output.reshape(text_rows, -1)
    gate_cols = jnp.repeat(jnp.tanh(cross_gate), HEAD_SIZE)
    return (self_output + gate_cols[None, :] * cross_output).astype(jnp.bfloat16)


def solution(mesh):
    placed = (
        P(("groups", "seq"), "head"),
        P(None, ("groups", "seq"), "head"),
        P(("groups", "seq")),
        P(("groups", "seq"), None),
        P(("groups", "seq"), None),
        P(None, ("groups", "seq"), "head"),
        P("head", None),
        P("seq", None, "head"),
        P("head"),
    )
    return jax.shard_map(
        per_device,
        mesh=mesh,
        in_specs=placed,
        out_specs=P(("groups", "seq"), "head"),
        check_vma=False,
    )
```

profile of v0, /device:TPU:8, one launch (start us, length us, event | category | flops | bytes accessed | tf_op | source)
XLA Modules:
  0.0 130.6 jit_solution(16018390959418832903)
XLA Ops:
  9.3 2.2 %fusion.38 = (f32[8,256]{1,0:T(8,128)S(1)}, f32[8,256,256]{1,2,0:T(8,128)}) fusion(bf16[256,8,80]{0,2,1:T(8,128)(2,1)S(1)} %bitcast.88, bf16[256,8,80]{0,2,1:T(8,128)(2,1)S(1)} %bitcast.87), kind=kOutput, calls=%fused_computation.70 | convolution fusion | flops 85459200 | bytes 2760704 | tf_op jit(solution)/shard_map/sub | solution.py:49
  11.5 1.9 %convolution_convert_fusion.1 = bf16[8,256,80]{1,2,0:T(8,128)(2,1)S(1)} fusion(bf16[256,8,80]{0,2,1:T(8,128)(2,1)S(1)} %bitcast.89, f32[8,256,256]{1,2,0:T(8,128)} %get-tuple-element.17, f32[8,256]{1,0:T(8,128)S(1)} %get-tuple-element.16), kind=kOutput, calls=%fused_computation.28 | convolution fusion | flops 85098496 | bytes 2760704 | tf_op jit(solution)/shard_map/hqk,khd->qhd/dot_general | solution.py:50
  13.4 1.8 %fusion.40 = f32[256,1280]{1,0:T(8,128)} fusion(bf16[256,640]{0,1:T(8,128)(2,1)S(1)} %bitcast.86, bf16[640,1280]{1,0:T(8,128)(2,1)S(1)} %copy-done), kind=kOutput, calls=%fused_computation.72 | convolution fusion | flops 419430400 | bytes 3276800 | tf_op jit(solution)/shard_map/dot_general | solution.py:54
  16.1 3.4 %collective-permute-start.2 = (s32[128]{0:T(128)S(1)}, s32[128]{0:T(128)S(1)}, u32[]{:S(2)}, u32[]{:S(2)}) collective-permute-start(s32[128]{0:T(128)S(1)} %copy-done.5), channel_id=1, source_target_pairs={{0,2},{2,4},{4,6},{6,8},{8,10},{10,12},{12,14},{1,3},{3,5},{5,7},{... | collective-permute-start | bytes 1544 | tf_op jit(solution)/shard_map/ppermute | solution.py:15
  19.7 3.5 %collective-permute-start = (bf16[2,128,512]{1,2,0:T(8,128)(2,1)S(1)}, bf16[2,128,512]{1,2,0:T(8,128)(2,1)S(1)}, u32[]{:S(2)}, u32[]{:S(2)}) collective-permute-start(bf16[2,128,512]{1,2,0:T(8,128)(2,1)S(1)} %copy.24), channel_id=1, source_target_pairs={{0,2},{2,4},{4,6},{6,8},{8,10},{10,12},{12,14},{1,3},{3,5},{5,7},{... | collective-permute-start | bytes 786440 | tf_op jit(solution)/shard_map/ppermute | solution.py:15
  23.5 3.4 %collective-permute-start.3 = (s32[128]{0:T(128)S(1)}, s32[128]{0:T(128)S(1)}, u32[]{:S(2)}, u32[]{:S(2)}) collective-permute-start(s32[128]{0:T(128)S(1)} %collective-permute-done.2), channel_id=1, source_target_pairs={{0,2},{2,4},{4,6},{6,8},{8,10},{10,12},{12,14},{1,3},{3,5},{5,7},{... | collective-permute-start | bytes 1544 | tf_op jit(solution)/shard_map/ppermute | solution.py:15
  26.9 1.5 %copy.52 = bf16[16,8,32,128]{3,2,1,0:T(8,128)(2,1)S(1)} copy(bf16[16,8,32,128]{3,1,2,0:T(8,128)(2,1)} %bitcast.83) | data formatting | bytes 2097152
  28.4 2.6 %collective-permute-done = bf16[2,128,512]{1,2,0:T(8,128)(2,1)S(1)} collective-permute-done((bf16[2,128,512]{1,2,0:T(8,128)(2,1)S(1)}, bf16[2,128,512]{1,2,0:T(8,128)(2,1)S(1)}, u32[]{:S(2)}, u32[]{:S(2)}) %collective-permute-start) | collective-permute-done | bytes 262176 | tf_op jit(solution)/shard_map/ppermute | solution.py:15
  30.9 3.1 %collective-permute-start.1 = (bf16[2,128,512]{1,2,0:T(8,128)(2,1)S(1)}, bf16[2,128,512]{1,2,0:T(8,128)(2,1)S(1)}, u32[]{:S(2)}, u32[]{:S(2)}) collective-permute-start(bf16[2,128,512]{1,2,0:T(8,128)(2,1)S(1)} %collective-permute-done), channel_id=1, source_target_pairs={{0,2},{2,4},{4,6},{6,8},{8,10},{10,12},{12,14},{1,3},{3,5},{5,7},{... | collective-permute-start | bytes 786440 | tf_op jit(solution)/shard_map/ppermute | solution.py:15
  34.2 12.1 %collective-permute-done.1 = bf16[2,128,512]{1,2,0:T(8,128)(2,1)S(1)} collective-permute-done((bf16[2,128,512]{1,2,0:T(8,128)(2,1)S(1)}, bf16[2,128,512]{1,2,0:T(8,128)(2,1)S(1)}, u32[]{:S(2)}, u32[]{:S(2)}) %collective-permute-start.1) | collective-permute-done | bytes 262176 | tf_op jit(solution)/shard_map/ppermute | solution.py:15
  48.4 3.7 %fusion.37 = (f32[4,8,128]{2,1,0:T(8,128)S(1)}, f32[4,8,128,384]{2,3,1,0:T(8,128)}) fusion(f32[4,384,128,8]{2,1,3,0:T(8,128)S(1)} %fusion.17, pred[128,384]{0,1:T(8,128)(4,1)S(1)} %and_and_fusion), kind=kOutput, calls=%fused_computation.69 | output fusion | flops 9437567 | bytes 12648448 | tf_op jit(solution)/shard_map/sub | solution.py:23
  52.1 1.6 %multiply_reduce_fusion.1 = f32[256]{0:T(256)S(1)} fusion(f32[256,1280]{1,0:T(8,128)} %all-reduce.2.cloned.1.call-done, bf16[256,1280]{1,0:T(8,128)(2,1)S(1)} %copy-done.1), kind=kLoop, calls=%fused_computation.25 | loop fusion | flops 1310464 | bytes 1967104 | tf_op jit(solution)/shard_map/reduce_sum | solution.py:57
  53.7 23.4 %all-gather.2.cloned.1.call-done = bf16[1280,2,512]{2,0,1:T(8,128)(2,1)} async-done(((bf16[160,2,512]{2,0,1:T(8,128)(2,1)}), bf16[1280,2,512]{2,0,1:T(8,128)(2,1)}) %all-gather.2.cloned.1.call-update) | async-done | bytes 2621456 | tf_op jit(solution)/shard_map/all_gather | solution.py:62
  77.1 3.9 %convolution_convert_fusion = bf16[256,2,512]{2,0,1:T(8,128)(2,1)} fusion(bf16[1280,2,512]{2,0,1:T(8,128)(2,1)} %all-gather.2.cloned.1.call-done, f32[256,1280]{1,0:T(8,128)} %all-reduce.2.cloned.1.call-done, bf16[256,1280]{1,0:T(8,128)(2,1)S(1)} %copy-done.1, f32[256]{0:T(256)S(1)} %add_rsqrt_fusion), kind=kOutput, calls=%fused_computation.27 | convolution fusion | flops 672661504 | bytes 5112832 | tf_op jit(solution)/shard_map/ic,cjf->ijf/dot_general | solution.py:59
  81.0 2.6 %collective-permute-start.4 = (bf16[256,2,512]{2,0,1:T(8,128)(2,1)}, bf16[256,2,512]{2,0,1:T(8,128)(2,1)S(1)}, u32[]{:S(2)}, u32[]{:S(2)}) collective-permute-start(bf16[256,2,512]{2,0,1:T(8,128)(2,1)} %convolution_convert_fusion), channel_id=1, source_target_pairs={{0,2},{2,4},{4,6},{6,8},{8,10},{10,12},{12,14},{1,3},{3,5},{5,7},{... | collective-permute-start | bytes 1572872 | tf_op jit(solution)/shard_map/ppermute | solution.py:15
  83.6 4.9 %fusion.11 = f32[4,128,8,128]{3,1,2,0:T(8,128)} fusion(bf16[384,4,128,1]{0,2,3,1:T(8,128)(2,1)S(1)} %bitcast.85, f32[4,8,128,384]{2,3,1,0:T(8,128)} %get-tuple-element.15, f32[4,8,128]{2,1,0:T(8,128)S(1)} %get-tuple-element.14), kind=kOutput, calls=%fused_computation.17 | convolution fusion | flops 405798912 | bytes 8798208 | tf_op jit(solution)/shard_map/ycmq,qyb->mycb/dot_general | solution.py:86
  88.5 2.9 %copy.39 = f32[128,4096]{1,0:T(8,128)} copy(f32[128,4096]{0,1:T(8,128)} %bitcast.81) | data formatting | bytes 4194304 | tf_op jit(solution)/shard_map/reshape | solution.py:92
  91.5 5.0 %collective-permute-done.4 = bf16[256,2,512]{2,0,1:T(8,128)(2,1)S(1)} collective-permute-done((bf16[256,2,512]{2,0,1:T(8,128)(2,1)}, bf16[256,2,512]{2,0,1:T(8,128)(2,1)S(1)}, u32[]{:S(2)}, u32[]{:S(2)}) %collective-permute-start.4) | collective-permute-done | bytes 524320 | tf_op jit(solution)/shard_map/ppermute | solution.py:15
  96.5 2.1 %pad_maximum_fusion.1 = (bf16[512,1,512]{2,0,1:T(8,128)(2,1)}, bf16[512,1,512]{2,0,1:T(8,128)(2,1)}) fusion(bf16[256,2,512]{2,0,1:T(8,128)(2,1)} %convolution_convert_fusion, bf16[256,2,512]{2,0,1:T(8,128)(2,1)S(1)} %collective-permute-done.4), kind=kLoop, calls=%fused_computation.40 | loop fusion | flops 2097152 | bytes 2097152 | tf_op jit(solution)/shard_map/concatenate | solution.py:93
  99.8 4.5 %fusion.15 = f32[4,512,128,8]{2,1,3,0:T(8,128)} fusion(bf16[128,4,8,128]{3,2,1,0:T(8,128)(2,1)S(1)} %bitcast.78, bf16[512,4,128,1]{2,1,0,3:T(4,128)(2,1)S(1)} %bitcast.79), kind=kOutput, calls=%fused_computation.32 | convolution fusion | flops 536870912 | bytes 9961472 | tf_op jit(solution)/shard_map/tgrd,kgd->grtk/dot_general | solution.py:19
  105.5 8.9 %fusion.39 = (f32[4,8,128]{2,1,0:T(8,128)S(1)}, f32[4,8,128,512]{2,3,1,0:T(8,128)S(1)}) fusion(f32[4,512,128,8]{2,1,3,0:T(8,128)} %fusion.15, pred[128,512]{0,1:T(8,128)(4,1)S(1)} %compare_and_fusion), kind=kOutput, calls=%fused_computation.71 | output fusion | flops 12583423 | bytes 16859136 | tf_op jit(solution)/shard_map/sub | solution.py:23
  114.4 2.3 %fusion.8 = f32[4,128,8,128]{3,1,2,0:T(8,128)} fusion(bf16[512,4,128,1]{0,2,3,1:T(8,128)(2,1)S(1)} %bitcast.84, f32[4,8,128,512]{2,3,1,0:T(8,128)S(1)} %get-tuple-element.19, f32[128]{0:T(128)S(1)} %compare_convert_fusion, f32[4,8,128]{2,1,0:T(8,128)S(1)} %get-tuple-element.18), kind=kOutput, calls=%fused_computation.14 | convolution fusion | flops 543162368 | bytes 11026944 | tf_op jit(solution)/shard_map/ycmq,qyb->mycb/dot_general | solution.py:106
  116.8 2.9 %copy.38 = f32[128,4096]{1,0:T(8,128)} copy(f32[128,4096]{0,1:T(8,128)} %bitcast.80) | data formatting | bytes 4194304 | tf_op jit(solution)/shard_map/reshape | solution.py:112
  119.7 3.5 %add_convert_fusion = bf16[128,4096]{1,0:T(8,128)(2,1)} fusion(f32[128,4096]{1,0:T(8,128)} %copy.39, f32[128,4096]{1,0:T(8,128)} %copy.38, f32[4096]{0:T(1024)S(1)} %broadcast_bitcast_fusion), kind=kLoop, calls=%fused_computation.19 | loop fusion | flops 1572864 | bytes 5259264 | tf_op jit(solution)/shard_map/convert_element_type | solution.py:114
  (46 shorter events, 7.8 us)
Async XLA Ops:
  7.4 6.0 %copy-start = (bf16[640,1280]{1,0:T(8,128)(2,1)S(1)}, bf16[640,1280]{1,0:T(8,128)(2,1)}, u32[]{:S(2)}) copy-start(bf16[640,1280]{1,0:T(8,128)(2,1)} %param.15) | copy-start | bytes 4915204
  7.4 44.7 %all-reduce.2.cloned.1.call-start = ((), (), s32[]{:S(2)}) async-start(), calls=%async_computation | async-start | bytes 2621440 | tf_op jit(solution)/shard_map/psum | solution.py:55
  13.4 1.9 %copy-start.3 = (bf16[160,2,512]{2,1,0:T(2,128)(2,1)S(1)}, bf16[160,2,512]{2,1,0:T(2,128)(2,1)}, u32[]{:S(2)}) copy-start(bf16[160,2,512]{2,1,0:T(2,128)(2,1)} %param.16) | copy-start | bytes 983044
  13.4 2.7 %copy-start.5 = (s32[128]{0:T(128)S(1)}, s32[128]{0:T(128)}, u32[]{:S(2)}) copy-start(s32[128]{0:T(128)} %param.11) | copy-start | bytes 1540
  13.4 6.1 %copy-start.4 = (bf16[2,128,512]{2,1,0:T(8,128)(2,1)S(1)}, bf16[2,128,512]{2,1,0:T(8,128)(2,1)}, u32[]{:S(2)}) copy-start(bf16[2,128,512]{2,1,0:T(8,128)(2,1)} %param.10) | copy-start | bytes 786436
  13.4 9.7 %copy-start.7 = (f32[32]{0:T(128)S(1)}, f32[32]{0:T(128)}, u32[]{:S(2)}) copy-start(f32[32]{0:T(128)} %param.17) | copy-start | bytes 388
  13.4 9.8 %copy-start.6 = (s32[128,2]{0,1:T(2,128)S(1)}, s32[128,2]{0,1:T(2,128)}, u32[]{:S(2)}) copy-start(s32[128,2]{0,1:T(2,128)} %param.12) | copy-start | bytes 3076
  15.2 61.9 %all-gather.2.cloned.1.call-start = ((), (), s32[]{:S(2)}) async-start(), calls=%async_computation.1 | async-start | bytes 2949120 | tf_op jit(solution)/shard_map/all_gather | solution.py:62
  16.1 7.4 %collective-permute-start.2 = (s32[128]{0:T(128)S(1)}, s32[128]{0:T(128)S(1)}, u32[]{:S(2)}, u32[]{:S(2)}) collective-permute-start(s32[128]{0:T(128)S(1)} %copy-done.5), channel_id=1, source_target_pairs={{0,2},{2,4},{4,6},{6,8},{8,10},{10,12},{12,14},{1,3},{3,5},{5,7},{... | collective-permute-start | bytes 1544 | tf_op jit(solution)/shard_map/ppermute | solution.py:15
  19.7 11.3 %collective-permute-start = (bf16[2,128,512]{1,2,0:T(8,128)(2,1)S(1)}, bf16[2,128,512]{1,2,0:T(8,128)(2,1)S(1)}, u32[]{:S(2)}, u32[]{:S(2)}) collective-permute-start(bf16[2,128,512]{1,2,0:T(8,128)(2,1)S(1)} %copy.24), channel_id=1, source_target_pairs={{0,2},{2,4},{4,6},{6,8},{8,10},{10,12},{12,14},{1,3},{3,5},{5,7},{... | collective-permute-start | bytes 786440 | tf_op jit(solution)/shard_map/ppermute | solution.py:15
  23.5 10.5 %collective-permute-start.3 = (s32[128]{0:T(128)S(1)}, s32[128]{0:T(128)S(1)}, u32[]{:S(2)}, u32[]{:S(2)}) collective-permute-start(s32[128]{0:T(128)S(1)} %collective-permute-done.2), channel_id=1, source_target_pairs={{0,2},{2,4},{4,6},{6,8},{8,10},{10,12},{12,14},{1,3},{3,5},{5,7},{... | collective-permute-start | bytes 1544 | tf_op jit(solution)/shard_map/ppermute | solution.py:15
  30.9 15.5 %collective-permute-start.1 = (bf16[2,128,512]{1,2,0:T(8,128)(2,1)S(1)}, bf16[2,128,512]{1,2,0:T(8,128)(2,1)S(1)}, u32[]{:S(2)}, u32[]{:S(2)}) collective-permute-start(bf16[2,128,512]{1,2,0:T(8,128)(2,1)S(1)} %collective-permute-done), channel_id=1, source_target_pairs={{0,2},{2,4},{4,6},{6,8},{8,10},{10,12},{12,14},{1,3},{3,5},{5,7},{... | collective-permute-start | bytes 786440 | tf_op jit(solution)/shard_map/ppermute | solution.py:15
  48.4 3.7 %copy-start.1 = (bf16[256,1280]{1,0:T(8,128)(2,1)S(1)}, bf16[256,1280]{1,0:T(8,128)(2,1)}, u32[]{:S(2)}) copy-start(bf16[256,1280]{1,0:T(8,128)(2,1)} %param.13) | copy-start | bytes 1966084
  77.1 6.5 %copy-start.2 = (bf16[1,384,512]{1,2,0:T(8,128)(2,1)S(1)}, bf16[1,384,512]{1,2,0:T(8,128)(2,1)}, u32[]{:S(2)}) copy-start(bf16[1,384,512]{1,2,0:T(8,128)(2,1)} %get-tuple-element.11) | copy-start | bytes 1179652
  81.0 15.5 %collective-permute-start.4 = (bf16[256,2,512]{2,0,1:T(8,128)(2,1)}, bf16[256,2,512]{2,0,1:T(8,128)(2,1)S(1)}, u32[]{:S(2)}, u32[]{:S(2)}) collective-permute-start(bf16[256,2,512]{2,0,1:T(8,128)(2,1)} %convolution_convert_fusion), channel_id=1, source_target_pairs={{0,2},{2,4},{4,6},{6,8},{8,10},{10,12},{12,14},{1,3},{3,5},{5,7},{... | collective-permute-start | bytes 1572872 | tf_op jit(solution)/shard_map/ppermute | solution.py:15
Sparse Core Ops, SparseCore 0:
  15.3 21.4 all-reduce.1
Sparse Core Ops, SparseCore 1:
  17.9 59.1 all-gather.1
where the time goes:
time: 131 us
  waiting for transfers between devices  43.2 us (33%)
  matrix products  22.5 us (17%)
  other arithmetic  20.2 us (15%)
  starting transfers between devices  16 us (12%)
  between operations  15.1 us (12%)
  local copies, waits for them, and re-layouts  13.6 us (10%)
    all_gather x1, waiting for transfers between devices, per_device(): lax.all_gather(cross_keyvalue_weight, 'seq', axis=0, tiled=True)  23.4 us
    ppermute x5, waiting for transfers between devices, passed_along(): return lax.ppermute(block, axis, route)  19.7 us
    ppermute x5, starting transfers between devices, passed_along(): return lax.ppermute(block, axis, route)  16 us
    sub x2, other arithmetic, attend_heads(): return jax.nn.softmax(scores, axis=-1)  12.6 us
    dot_general x2, matrix products, attend_heads(): jnp.einsum('tgrd,kgd->grtk', query_rows, keys, preferred_element_type=jnp...  5.54 us
    dot_general x1, matrix products, per_device(): jnp.einsum('ycmq,qyb->mycb', self_attention_weights, all_keyval[1].reshap...  4.89 us
    dot_general x1, matrix products, per_device(): jnp.einsum('ic,cjf->ijf', image_norm, lax.all_gather(cross_keyvalue_weigh...  3.87 us
    convert_element_type x1, other arithmetic, per_device(): (self_output + gate_cols[None, :] * cross_output).astype(jnp.bfloat16)  3.46 us
  transfers between devices with their start and end apart: 7, of which 4 were waited for; matrix products, arithmetic and copies ran while one was open for 14% of the time, Pallas kernels for 0%

commit v1 on v0

--- a/solution.py
+++ b/solution.py
@@ -7,6 +7,18 @@
 HEAD_SIZE = 128
 VHD = 80
 WINDOW_BLOCKS = 2
+
+
+def collect(x, axis, dim):
+    ways, here, step = (lax.axis_size(axis), lax.axis_index(axis), x.shape[dim])
+    line, have = (x, 1)
+    while have < ways:
+        line = jnp.concatenate(
+            [line, lax.ppermute(line, axis, [(d, (d - have) % ways) for d in range(ways)])],
+            axis=dim,
+        )
+        have = 2 * have
+    return jnp.roll(line, here * step, axis=dim)
 
 
 def passed_along(block, axis, distance):
@@ -59,7 +71,7 @@
     image_key_value = jnp.einsum(
         "ic,cjf->ijf",
         image_norm,
-        lax.all_gather(cross_keyvalue_weight, "seq", axis=0, tiled=True),
+        collect(cross_keyvalue_weight, "seq", 0),
         preferred_element_type=jnp.float32,
     ).astype(jnp.bfloat16)
     earlier_tile = passed_along(image_key_value, "seq", 1)

time: 131 us -> 169 us (1.29)
  waiting for transfers between devices: 43.2 us -> 68.7 us
  local copies, waits for them, and re-layouts: 13.6 us -> 22.6 us
  starting transfers between devices: 16 us -> 22.5 us
  matrix products: 22.5 us -> 19.8 us
    ppermute x0 -> x3, waiting for transfers between devices: none -> 50.7 us  [collect(): lax.ppermute(line, axis, [(d, (d - have) % ways) for d in range(ways)])]
    all_gather x1 -> x0, waiting for transfers between devices: 23.4 us -> none  [per_device(): lax.all_gather(cross_keyvalue_weight, 'seq', axis=0, tiled=True)]
    unnamed x19 -> x35, local copies, waits for them, and re-layouts: 2.45 us -> 10.2 us
    ppermute x0 -> x3, starting transfers between devices: none -> 4.22 us  [collect(): lax.ppermute(line, axis, [(d, (d - have) % ways) for d in range(ways)])]
    dot_general x1, matrix products: 4.89 us -> 2.11 us  [per_device(): jnp.einsum('ycmq,qyb->mycb', self_attention_weights, all_keyval[1].reshap...]
    concatenate x0 -> x1, local copies, waits for them, and re-layouts: none -> 2.62 us  [collect(): return jnp.roll(line, here * step, axis=dim)]
    ppermute x5, starting transfers between devices: 16 us -> 18.3 us  [passed_along(): return lax.ppermute(block, axis, route)]
    concatenate x1, other arithmetic: 2.08 us -> 0.07 us  [per_device(): image_all = jnp.concatenate([earlier_tile, image_key_value], axis=0)]
  transfers between devices with their start and end apart: 7 -> 9, of which waited for: 4 -> 5; matrix products, arithmetic and copies ran while one was open for 14% -> 17% of each run, Pallas kernels for 0% -> 0%
where the time goes in v1:
time: 169 us; the launch traced here: 168 us
  waiting for transfers between devices  68.7 us (41%)
  local copies, waits for them, and re-layouts  22.6 us (13%)
  starting transfers between devices  22.5 us (13%)
  other arithmetic  20.5 us (12%)
  matrix products  19.8 us (12%)
  between operations  13.7 us (8%)
    ppermute x3, waiting for transfers between devices, collect(): lax.ppermute(line, axis, [(d, (d - have) % ways) for d in range(ways)])  50.7 us
    ppermute x5, starting transfers between devices, passed_along(): return lax.ppermute(block, axis, route)  18.3 us
    ppermute x5, waiting for transfers between devices, passed_along(): return lax.ppermute(block, axis, route)  17.9 us
    sub x2, other arithmetic, attend_heads(): return jax.nn.softmax(scores, axis=-1)  12.5 us
    unnamed x35, local copies, waits for them, and re-layouts  10.2 us
    dot_general x2, matrix products, attend_heads(): jnp.einsum('tgrd,kgd->grtk', query_rows, keys, preferred_element_type=jnp...  5.54 us
    ppermute x3, starting transfers between devices, collect(): lax.ppermute(line, axis, [(d, (d - have) % ways) for d in range(ways)])  4.22 us
    convert_element_type x1, other arithmetic, per_device(): (self_output + gate_cols[None, :] * cross_output).astype(jnp.bfloat16)  3.46 us
  transfers between devices with their start and end apart: 9, of which 5 were waited for; matrix products, arithmetic and copies ran while one was open for 17% of the time, Pallas kernels for 0%

profile of v1, /device:TPU:8, one launch (start us, length us, event | category | flops | bytes accessed | tf_op | source)
XLA Modules:
  0.0 167.8 jit_solution(5102160903002249379)
XLA Ops:
  12.4 3.2 %fusion.45 = (f32[8,256]{1,0:T(8,128)S(1)}, f32[8,256,256]{1,2,0:T(8,128)}) fusion(bf16[256,8,80]{0,2,1:T(8,128)(2,1)S(1)} %bitcast.87, bf16[256,8,80]{0,2,1:T(8,128)(2,1)} %bitcast.86), kind=kOutput, calls=%fused_computation.84 | convolution fusion | flops 85459200 | bytes 2760704 | tf_op jit(solution)/shard_map/sub | solution.py:61
  15.5 1.9 %convolution_convert_fusion = bf16[8,256,80]{1,2,0:T(8,128)(2,1)S(1)} fusion(bf16[256,8,80]{0,2,1:T(8,128)(2,1)S(1)} %bitcast.88, f32[8,256,256]{1,2,0:T(8,128)} %get-tuple-element.19, f32[8,256]{1,0:T(8,128)S(1)} %get-tuple-element.18), kind=kOutput, calls=%fused_computation.31 | convolution fusion | flops 85098496 | bytes 2760704 | tf_op jit(solution)/shard_map/hqk,khd->qhd/dot_general | solution.py:62
  19.3 2.5 %collective-permute-start.2 = (s32[128]{0:T(128)S(1)}, s32[128]{0:T(128)S(1)}, u32[]{:S(2)}, u32[]{:S(2)}) collective-permute-start(s32[128]{0:T(128)S(1)} %copy-done.8), channel_id=1, source_target_pairs={{0,2},{2,4},{4,6},{6,8},{8,10},{10,12},{12,14},{1,3},{3,5},{5,7},{... | collective-permute-start | bytes 1544 | tf_op jit(solution)/shard_map/ppermute | solution.py:27
  22.0 4.3 %collective-permute-start = (bf16[2,128,512]{1,2,0:T(8,128)(2,1)S(1)}, bf16[2,128,512]{1,2,0:T(8,128)(2,1)S(1)}, u32[]{:S(2)}, u32[]{:S(2)}) collective-permute-start(bf16[2,128,512]{1,2,0:T(8,128)(2,1)S(1)} %copy.28), channel_id=1, source_target_pairs={{0,2},{2,4},{4,6},{6,8},{8,10},{10,12},{12,14},{1,3},{3,5},{5,7},{... | collective-permute-start | bytes 786440 | tf_op jit(solution)/shard_map/ppermute | solution.py:27
  27.9 2.5 %collective-permute-start.3 = (s32[128]{0:T(128)S(1)}, s32[128]{0:T(128)S(1)}, u32[]{:S(2)}, u32[]{:S(2)}) collective-permute-start(s32[128]{0:T(128)S(1)} %collective-permute-done.2), channel_id=1, source_target_pairs={{0,2},{2,4},{4,6},{6,8},{8,10},{10,12},{12,14},{1,3},{3,5},{5,7},{... | collective-permute-start | bytes 1544 | tf_op jit(solution)/shard_map/ppermute | solution.py:27
  31.9 2.3 %collective-permute-done.3 = s32[128]{0:T(128)S(1)} collective-permute-done((s32[128]{0:T(128)S(1)}, s32[128]{0:T(128)S(1)}, u32[]{:S(2)}, u32[]{:S(2)}) %collective-permute-start.3) | collective-permute-done | bytes 544 | tf_op jit(solution)/shard_map/ppermute | solution.py:27
  34.2 2.0 %collective-permute-start.1 = (bf16[2,128,512]{1,2,0:T(8,128)(2,1)S(1)}, bf16[2,128,512]{1,2,0:T(8,128)(2,1)S(1)}, u32[]{:S(2)}, u32[]{:S(2)}) collective-permute-start(bf16[2,128,512]{1,2,0:T(8,128)(2,1)S(1)} %collective-permute-done), channel_id=1, source_target_pairs={{0,2},{2,4},{4,6},{6,8},{8,10},{10,12},{12,14},{1,3},{3,5},{5,7},{... | collective-permute-start | bytes 786440 | tf_op jit(solution)/shard_map/ppermute | solution.py:27
  37.8 8.5 %collective-permute-done.1 = bf16[2,128,512]{1,2,0:T(8,128)(2,1)S(1)} collective-permute-done((bf16[2,128,512]{1,2,0:T(8,128)(2,1)S(1)}, bf16[2,128,512]{1,2,0:T(8,128)(2,1)S(1)}, u32[]{:S(2)}, u32[]{:S(2)}) %collective-permute-start.1) | collective-permute-done | bytes 262176 | tf_op jit(solution)/shard_map/ppermute | solution.py:27
  47.2 4.2 %collective-permute-done.5 = bf16[320,2,512]{2,0,1:T(8,128)(2,1)S(1)} collective-permute-done((bf16[320,2,512]{2,0,1:T(8,128)(2,1)S(1)}, bf16[320,2,512]{2,0,1:T(8,128)(2,1)S(1)}, u32[]{:S(2)}, u32[]{:S(2)}) %collective-permute-start.5) | collective-permute-done | bytes 655392 | tf_op jit(solution)/shard_map/ppermute | solution.py:17
  52.6 2.3 %collective-permute-start.6 = (bf16[640,2,512]{2,0,1:T(8,128)(2,1)}, bf16[640,2,512]{2,0,1:T(8,128)(2,1)}, u32[]{:S(2)}, u32[]{:S(2)}) collective-permute-start(bf16[640,2,512]{2,0,1:T(8,128)(2,1)} %pad_maximum_fusion), channel_id=1, source_target_pairs={{0,8},{2,10},{4,12},{6,14},{8,0},{10,2},{12,4},{14,6},{1,9},{3,11}... | collective-permute-start | bytes 3932168 | tf_op jit(solution)/shard_map/ppermute | solution.py:17
  56.0 3.6 %fusion.44 = (f32[4,8,128]{2,1,0:T(8,128)S(1)}, f32[4,8,128,384]{2,3,1,0:T(8,128)}) fusion(f32[4,384,128,8]{2,1,3,0:T(8,128)S(1)} %fusion.22, pred[128,384]{0,1:T(8,128)(4,1)S(1)} %and_and_fusion), kind=kOutput, calls=%fused_computation.83 | output fusion | flops 9437567 | bytes 12648448 | tf_op jit(solution)/shard_map/sub | solution.py:35
  62.1 46.5 %collective-permute-done.6 = bf16[640,2,512]{2,0,1:T(8,128)(2,1)} collective-permute-done((bf16[640,2,512]{2,0,1:T(8,128)(2,1)}, bf16[640,2,512]{2,0,1:T(8,128)(2,1)}, u32[]{:S(2)}, u32[]{:S(2)}) %collective-permute-start.6) | collective-permute-done | bytes 1310752 | tf_op jit(solution)/shard_map/ppermute | solution.py:17
  108.6 2.5 %constant_dynamic-update-slice_fusion.4 = bf16[2560,2,512]{2,0,1:T(8,128)(2,1)} fusion(bf16[2560,2,512]{2,0,1:T(8,128)(2,1)} %constant_dynamic-update-slice_fusion.5, bf16[640,2,512]{2,0,1:T(8,128)(2,1)} %collective-permute-done.6), kind=kLoop, calls=%fused_computation.53 | loop fusion | bytes 2621440
  113.5 2.6 %constant_dynamic-update-slice_fusion = bf16[2560,2,512]{2,0,1:T(8,128)(2,1)} fusion(bf16[2560,2,512]{2,0,1:T(8,128)(2,1)} %constant_dynamic-update-slice_fusion.1, bf16[640,2,512]{2,0,1:T(8,128)(2,1)} %collective-permute-done.6), kind=kLoop, calls=%fused_computation.49 | loop fusion | bytes 2621440 | tf_op jit(solution)/shard_map/jit(_roll_dynamic)/concatenate | solution.py:21
  116.2 2.9 %fusion.16 = bf16[256,2,512]{2,0,1:T(8,128)(2,1)S(1)} fusion(bf16[2560,2,512]{2,0,1:T(8,128)(2,1)} %constant_dynamic-update-slice_fusion, s32[]{:T(128)S(6)} %select_n.32, f32[256,1280]{1,0:T(8,128)S(1)} %copy-done.2, bf16[256,1280]{1,0:T(8,128)(2,1)S(1)} %copy-done.3, f32[256]{0:T(256)S(1)} %add_rsqrt_fusion), kind=kOutput, calls=%fused_computation.30 | convolution fusion | flops 672661504 | bytes 5112836 | tf_op jit(solution)/shard_map/ic,cjf->ijf/dot_general | solution.py:71
  119.1 6.9 %collective-permute-start.7 = (bf16[256,2,512]{2,0,1:T(8,128)(2,1)S(1)}, bf16[256,2,512]{2,0,1:T(8,128)(2,1)S(1)}, u32[]{:S(2)}, u32[]{:S(2)}) collective-permute-start(bf16[256,2,512]{2,0,1:T(8,128)(2,1)S(1)} %fusion.16), channel_id=1, source_target_pairs={{0,2},{2,4},{4,6},{6,8},{8,10},{10,12},{12,14},{1,3},{3,5},{5,7},{... | collective-permute-start | bytes 1572872 | tf_op jit(solution)/shard_map/ppermute | solution.py:27
  126.0 2.1 %fusion.11 = f32[4,128,8,128]{3,1,2,0:T(8,128)} fusion(bf16[384,4,128,1]{0,2,3,1:T(8,128)(2,1)S(1)} %bitcast.84, f32[4,8,128,384]{2,3,1,0:T(8,128)S(1)} %copy-done.12, f32[4,8,128]{2,1,0:T(8,128)S(1)} %get-tuple-element.16), kind=kOutput, calls=%fused_computation.17 | convolution fusion | flops 405798912 | bytes 8798208 | tf_op jit(solution)/shard_map/ycmq,qyb->mycb/dot_general | solution.py:98
  128.1 2.9 %copy.47 = f32[128,4096]{1,0:T(8,128)} copy(f32[128,4096]{0,1:T(8,128)} %bitcast.80) | data formatting | bytes 4194304 | tf_op jit(solution)/shard_map/reshape | solution.py:104
  131.1 7.1 %collective-permute-done.7 = bf16[256,2,512]{2,0,1:T(8,128)(2,1)S(1)} collective-permute-done((bf16[256,2,512]{2,0,1:T(8,128)(2,1)S(1)}, bf16[256,2,512]{2,0,1:T(8,128)(2,1)S(1)}, u32[]{:S(2)}, u32[]{:S(2)}) %collective-permute-start.7) | collective-permute-done | bytes 524320 | tf_op jit(solution)/shard_map/ppermute | solution.py:27
  138.4 4.5 %fusion.20 = f32[4,512,128,8]{2,1,3,0:T(8,128)} fusion(bf16[128,4,8,128]{3,2,1,0:T(8,128)(2,1)S(1)} %bitcast.77, bf16[512,4,128,1]{2,1,0,3:T(4,128)(2,1)S(1)} %bitcast.78), kind=kOutput, calls=%fused_computation.35 | convolution fusion | flops 536870912 | bytes 9961472 | tf_op jit(solution)/shard_map/tgrd,kgd->grtk/dot_general | solution.py:31
  143.2 8.9 %fusion.46 = (f32[4,8,128]{2,1,0:T(8,128)S(1)}, f32[4,8,128,512]{2,3,1,0:T(8,128)S(1)}) fusion(f32[4,512,128,8]{2,1,3,0:T(8,128)} %fusion.20, pred[128,512]{0,1:T(8,128)(4,1)S(1)} %copy-done.7), kind=kOutput, calls=%fused_computation.85 | output fusion | flops 12583423 | bytes 16859136 | tf_op jit(solution)/shard_map/sub | solution.py:35
  152.1 2.3 %fusion.8 = f32[4,128,8,128]{3,1,2,0:T(8,128)} fusion(bf16[512,4,128,1]{0,2,3,1:T(8,128)(2,1)S(1)} %bitcast.83, f32[4,8,128,512]{2,3,1,0:T(8,128)S(1)} %get-tuple-element.21, f32[128]{0:T(128)S(1)} %copy-done.11, f32[4,8,128]{2,1,0:T(8,128)S(1)} %get-tuple-element.20), kind=kOutput, calls=%fused_computation.14 | convolution fusion | flops 543162368 | bytes 11026944 | tf_op jit(solution)/shard_map/ycmq,qyb->mycb/dot_general | solution.py:118
  154.4 3.1 %copy.46 = f32[128,4096]{1,0:T(8,128)} copy(f32[128,4096]{0,1:T(8,128)} %bitcast.79) | data formatting | bytes 4194304 | tf_op jit(solution)/shard_map/reshape | solution.py:124
  157.5 3.5 %add_convert_fusion = bf16[128,4096]{1,0:T(8,128)(2,1)} fusion(f32[128,4096]{1,0:T(8,128)} %copy.47, f32[128,4096]{1,0:T(8,128)} %copy.46, f32[4096]{0:T(1024)S(1)} %broadcast_bitcast_fusion), kind=kLoop, calls=%fused_computation.21 | loop fusion | flops 1572864 | bytes 5259264 | tf_op jit(solution)/shard_map/convert_element_type | solution.py:126
  (68 shorter events, 20.7 us)
Async XLA Ops:
  6.5 11.0 %copy-start = (bf16[640,1280]{1,0:T(8,128)(2,1)S(1)}, bf16[640,1280]{1,0:T(8,128)(2,1)}, u32[]{:S(2)}) copy-start(bf16[640,1280]{1,0:T(8,128)(2,1)} %param.15) | copy-start | bytes 4915204
  6.5 54.0 %all-reduce.2.cloned.1.call-start = ((), (), s32[]{:S(2)}) async-start(), calls=%async_computation | async-start | bytes 2621440 | tf_op jit(solution)/shard_map/psum | solution.py:67
  8.5 27.8 %collective-permute-start.4 = (bf16[160,2,512]{2,0,1:T(8,128)(2,1)S(1)}, bf16[160,2,512]{2,0,1:T(8,128)(2,1)S(1)}, u32[]{:S(2)}, u32[]{:S(2)}) collective-permute-start(bf16[160,2,512]{2,0,1:T(8,128)(2,1)S(1)} %get-tuple-element.12), channel_id=1, source_target_pairs={{0,14},{2,0},{4,2},{6,4},{8,6},{10,8},{12,10},{14,12},{1,15},{3,1}... | collective-permute-start | bytes 983048 | tf_op jit(solution)/shard_map/ppermute | solution.py:17
  15.5 3.8 %copy-start.8 = (s32[128]{0:T(128)S(1)}, s32[128]{0:T(128)}, u32[]{:S(2)}) copy-start(s32[128]{0:T(128)} %param.11) | copy-start | bytes 1540
  15.5 6.3 %copy-start.6 = (bf16[2,128,512]{2,1,0:T(8,128)(2,1)S(1)}, bf16[2,128,512]{2,1,0:T(8,128)(2,1)}, u32[]{:S(2)}) copy-start(bf16[2,128,512]{2,1,0:T(8,128)(2,1)} %param.10) | copy-start | bytes 786436
  17.5 8.9 %copy-start.9 = (s32[128,2]{0,1:T(2,128)S(1)}, s32[128,2]{0,1:T(2,128)}, u32[]{:S(2)}) copy-start(s32[128,2]{0,1:T(2,128)} %param.12) | copy-start | bytes 3076
  17.5 9.5 %copy-start.10 = (f32[32]{0:T(128)S(1)}, f32[32]{0:T(128)}, u32[]{:S(2)}) copy-start(f32[32]{0:T(128)} %param.17) | copy-start | bytes 388
  19.3 8.6 %collective-permute-start.2 = (s32[128]{0:T(128)S(1)}, s32[128]{0:T(128)S(1)}, u32[]{:S(2)}, u32[]{:S(2)}) collective-permute-start(s32[128]{0:T(128)S(1)} %copy-done.8), channel_id=1, source_target_pairs={{0,2},{2,4},{4,6},{6,8},{8,10},{10,12},{12,14},{1,3},{3,5},{5,7},{... | collective-permute-start | bytes 1544 | tf_op jit(solution)/shard_map/ppermute | solution.py:27
  22.0 12.2 %collective-permute-start = (bf16[2,128,512]{1,2,0:T(8,128)(2,1)S(1)}, bf16[2,128,512]{1,2,0:T(8,128)(2,1)S(1)}, u32[]{:S(2)}, u32[]{:S(2)}) collective-permute-start(bf16[2,128,512]{1,2,0:T(8,128)(2,1)S(1)} %copy.28), channel_id=1, source_target_pairs={{0,2},{2,4},{4,6},{6,8},{8,10},{10,12},{12,14},{1,3},{3,5},{5,7},{... | collective-permute-start | bytes 786440 | tf_op jit(solution)/shard_map/ppermute | solution.py:27
  27.9 6.3 %collective-permute-start.3 = (s32[128]{0:T(128)S(1)}, s32[128]{0:T(128)S(1)}, u32[]{:S(2)}, u32[]{:S(2)}) collective-permute-start(s32[128]{0:T(128)S(1)} %collective-permute-done.2), channel_id=1, source_target_pairs={{0,2},{2,4},{4,6},{6,8},{8,10},{10,12},{12,14},{1,3},{3,5},{5,7},{... | collective-permute-start | bytes 1544 | tf_op jit(solution)/shard_map/ppermute | solution.py:27
  34.2 12.0 %collective-permute-start.1 = (bf16[2,128,512]{1,2,0:T(8,128)(2,1)S(1)}, bf16[2,128,512]{1,2,0:T(8,128)(2,1)S(1)}, u32[]{:S(2)}, u32[]{:S(2)}) collective-permute-start(bf16[2,128,512]{1,2,0:T(8,128)(2,1)S(1)} %collective-permute-done), channel_id=1, source_target_pairs={{0,2},{2,4},{4,6},{6,8},{8,10},{10,12},{12,14},{1,3},{3,5},{5,7},{... | collective-permute-start | bytes 786440 | tf_op jit(solution)/shard_map/ppermute | solution.py:27
  36.3 15.1 %collective-permute-start.5 = (bf16[320,2,512]{2,0,1:T(8,128)(2,1)S(1)}, bf16[320,2,512]{2,0,1:T(8,128)(2,1)S(1)}, u32[]{:S(2)}, u32[]{:S(2)}) collective-permute-start(bf16[320,2,512]{2,0,1:T(8,128)(2,1)S(1)} %pad_maximum_fusion.2), channel_id=1, source_target_pairs={{0,12},{2,14},{4,0},{6,2},{8,4},{10,6},{12,8},{14,10},{1,13},{3,15... | collective-permute-start | bytes 1966088 | tf_op jit(solution)/shard_map/ppermute | solution.py:17
  52.6 56.0 %collective-permute-start.6 = (bf16[640,2,512]{2,0,1:T(8,128)(2,1)}, bf16[640,2,512]{2,0,1:T(8,128)(2,1)}, u32[]{:S(2)}, u32[]{:S(2)}) collective-permute-start(bf16[640,2,512]{2,0,1:T(8,128)(2,1)} %pad_maximum_fusion), channel_id=1, source_target_pairs={{0,8},{2,10},{4,12},{6,14},{8,0},{10,2},{12,4},{14,6},{1,9},{3,11}... | collective-permute-start | bytes 3932168 | tf_op jit(solution)/shard_map/ppermute | solution.py:17
  56.0 4.6 %copy-start.3 = (bf16[256,1280]{1,0:T(8,128)(2,1)S(1)}, bf16[256,1280]{1,0:T(8,128)(2,1)}, u32[]{:S(2)}) copy-start(bf16[256,1280]{1,0:T(8,128)(2,1)} %param.13) | copy-start | bytes 1966084
  59.6 51.5 %copy-start.4 = (bf16[160,2,512]{2,1,0:T(2,128)(2,1)S(1)}, bf16[160,2,512]{2,1,0:T(2,128)(2,1)}, u32[]{:S(2)}) copy-start(bf16[160,2,512]{2,1,0:T(2,128)(2,1)} %param.16) | copy-start | bytes 983044
  62.1 54.1 %copy-start.2 = (f32[256,1280]{1,0:T(8,128)S(1)}, f32[256,1280]{1,0:T(8,128)}, u32[]{:S(2)}) copy-start(f32[256,1280]{1,0:T(8,128)} %all-reduce.2.cloned.1.call-done) | copy-start | bytes 3932164
  113.5 12.5 %copy-start.5 = (bf16[1,384,512]{1,2,0:T(8,128)(2,1)S(1)}, bf16[1,384,512]{1,2,0:T(8,128)(2,1)}, u32[]{:S(2)}) copy-start(bf16[1,384,512]{1,2,0:T(8,128)(2,1)} %get-tuple-element.11) | copy-start | bytes 1179652
  113.5 12.5 %copy-start.12 = (f32[4,8,128,384]{2,3,1,0:T(8,128)S(1)}, f32[4,8,128,384]{2,3,1,0:T(8,128)}, u32[]{:S(2)}) copy-start(f32[4,8,128,384]{2,3,1,0:T(8,128)} %get-tuple-element.17) | copy-start | bytes 18874372
  119.1 19.1 %collective-permute-start.7 = (bf16[256,2,512]{2,0,1:T(8,128)(2,1)S(1)}, bf16[256,2,512]{2,0,1:T(8,128)(2,1)S(1)}, u32[]{:S(2)}, u32[]{:S(2)}) collective-permute-start(bf16[256,2,512]{2,0,1:T(8,128)(2,1)S(1)} %fusion.16), channel_id=1, source_target_pairs={{0,2},{2,4},{4,6},{6,8},{8,10},{10,12},{12,14},{1,3},{3,5},{5,7},{... | collective-permute-start | bytes 1572872 | tf_op jit(solution)/shard_map/ppermute | solution.py:27
  138.4 4.7 %copy-start.7 = (pred[128,512]{0,1:T(8,128)(4,1)S(1)}, pred[128,512]{0,1:T(8,128)(4,1)}, u32[]{:S(2)}) copy-start(pred[128,512]{0,1:T(8,128)(4,1)} %compare_and_fusion) | copy-start | bytes 196612
  143.2 8.9 %copy-start.11 = (f32[128]{0:T(128)S(1)}, f32[128]{0:T(128)}, u32[]{:S(2)}) copy-start(f32[128]{0:T(128)} %compare_convert_fusion) | copy-start | bytes 1540
  154.4 6.5 %copy-start.1 = (bf16[640,1280]{1,0:T(8,128)(2,1)S(1)}, bf16[640,1280]{1,0:T(8,128)(2,1)}, u32[]{:S(2)}) copy-start(bf16[640,1280]{1,0:T(8,128)(2,1)} %param.15) | copy-start | bytes 4915204
Sparse Core Ops, SparseCore 0:
  19.4 20.5 all-reduce.1
